TPU v7x, 32 devices: a whole 2x2x4 slice. The times are simulated.
32 devices in a mesh: groups: 2 (over y), date: 4 (over z), tile: 2 (over x), head: 2 (over core).
Axes of the slice: x: 2, y: 2, z: 4, core: 2. Of those that a mesh axis runs over, the one named last changes fastest.
Arguments:
- tokens: bfloat16 [8, 8, 8, 64, 256], P('groups', 'tile', None, 'date'), parts along dimension 0, may hold values from -240 to 240
- cloud_mask: int32 [8, 8, 8, 64], P('groups', 'tile', None, 'date'), parts along dimension 0, may hold values from 0 to 1, as said below
- day_of_year: int32 [128], P(('groups', 'date')), parts along dimension 0, may hold values from 0 to 1460
- query: float32 [256], P('head'), may hold values from -6 to 6
- key_weight: bfloat16 [256, 256], P(None, 'head'), may hold values from -0.375 to 0.375
- value_weight: bfloat16 [256, 256], P(None, 'head'), may hold values from -0.375 to 0.375
- conv_first: bfloat16 [3, 3, 256, 256], P(None, None, None, 'head'), may hold values from -0.375 to 0.375
- conv_second: bfloat16 [3, 3, 256, 256], P(None, None, None, 'head'), may hold values from -0.1875 to 0.1875
Outputs:
- feature_map: bfloat16 [8, 8, 8, 256], P(('groups', 'date'), 'tile', None, 'head'), parts along dimension 0
There are 2 independent parts, one for each index of `groups`. A program takes and returns all parts, laid end to end along the dimension named above; an argument that names none is the same for every part. Nothing has to cross between parts.
Inputs may be any that keep to these rules, and one draw needn't show every extreme that they name: `cloud_mask`: a pixel may be clouded on all 64 dates.
All inputs are finite; a program needn't handle non-finite values.
Results may differ from a plain program's by a relative error of at most 0.012.
The roundings to bfloat16 on the way count: a program that leaves them out, or rounds other values in their place, can miss the bound.
Values may be sent and summed in bfloat16 or wider, within the bound.
A program may use at most 128 MiB of HBM per device.

v0:
```python
import jax
import jax.numpy as jnp
from jax import lax
from jax.sharding import PartitionSpec as P

HSIZE = 32
TILE_DEV = 1
cloud_penalty = 6.0


def with_halo(block, sides, width):
    for axis, dim in sides:
        count = lax.axis_size(axis)
        forward = [(i, i + 1) for i in range(count - 1)]
        backward = [(target, source) for source, target in forward]
        low = lax.ppermute(
            lax.slice_in_dim(block, block.shape[dim] - width, None, axis=dim), axis, forward
        )
        high = lax.ppermute(lax.slice_in_dim(block, 0, width, axis=dim), axis, backward)
        block = jnp.concatenate([low, block, high], axis=dim)
    return block


def encoding(day_of_year, width):
    chan = jnp.arange(width)
    expo = (2 * (chan // 2)).astype(jnp.float32) / width
    freq = jnp.power(jnp.float32(1000.0), -expo)
    angle = day_of_year.astype(jnp.float32)[:, None] * freq[None, :]
    return jnp.where((chan % 2 == 0)[None, :], jnp.sin(angle), jnp.cos(angle))


def widen(scales):
    return jnp.repeat(scales, HSIZE, axis=-1)


def merge_blocks(tops, tots, parts):
    best = jnp.max(tops, axis=0)
    scales = jnp.exp(tops - best[None])
    own_totals = jnp.sum(tots * scales, axis=0)
    own_sums = jnp.sum(parts * widen(scales), axis=0)
    return (own_totals, own_sums)


def convolve(block, kernel):
    rows, cols = (block.shape[1], block.shape[2])
    padded = with_halo(block, (("tile", 1),), 1)
    whole = lax.all_gather(padded, "head", axis=3, tiled=True)
    whole = jnp.pad(whole, ((0, 0), (0, 0), (1, 1), (0, 0)))
    total = jnp.zeros((block.shape[0] * rows * cols, kernel.shape[3]), jnp.float32)
    for arow in range(3):
        for bcol in range(3):
            piece = whole[:, arow : arow + rows, bcol : bcol + cols, :].reshape(-1, whole.shape[3])
            total = total + jnp.dot(piece, kernel[arow, bcol], preferred_element_type=jnp.float32)
    return total.reshape(block.shape[0], rows, cols, kernel.shape[3])


def local(
    tokens, cloud_mask, day_of_year, query, key_weight, value_weight, conv_first, conv_second
):
    tiles, rows, cols, dates, width = tokens.shape
    heads_dev = query.shape[0] // HSIZE
    table = encoding(day_of_year, width)
    inputs = (
        (tokens.astype(jnp.float32) + table[None, None, None])
        .astype(jnp.bfloat16)
        .reshape(-1, width)
    )
    keys = jnp.dot(inputs, key_weight, preferred_element_type=jnp.float32).reshape(
        tiles, rows, cols, dates, heads_dev, HSIZE
    )
    vals = jnp.dot(inputs, value_weight, preferred_element_type=jnp.float32).reshape(
        tiles, rows, cols, dates, heads_dev, HSIZE
    )
    query_heads = query.reshape(heads_dev, HSIZE)
    score = jnp.sum(keys * query_heads, axis=-1) / jnp.sqrt(jnp.float32(HSIZE))
    score = score - cloud_penalty * (1.0 - cloud_mask[..., None].astype(jnp.float32))
    top = jnp.max(score, axis=3)
    expo = jnp.exp(score - top[:, :, :, None, :])
    totals = jnp.sum(expo, axis=3)
    sums = jnp.sum(expo[..., None] * vals, axis=3).reshape(tiles, rows, cols, heads_dev * HSIZE)
    got = (
        lax.all_to_all(top, "date", split_axis=0, concat_axis=0, tiled=True),
        lax.all_to_all(totals, "date", split_axis=0, concat_axis=0, tiled=True),
        lax.all_to_all(sums, "date", split_axis=0, concat_axis=0, tiled=True),
    )
    sources = got[0].shape[0] // TILE_DEV
    tops = got[0].reshape(sources, TILE_DEV, rows, cols, heads_dev)
    tots = got[1].reshape(sources, TILE_DEV, rows, cols, heads_dev)
    parts = got[2].reshape(sources, TILE_DEV, rows, cols, heads_dev * HSIZE)
    own_totals, own_sums = merge_blocks(tops, tots, parts)
    pooled = (own_sums / widen(own_totals)).astype(jnp.bfloat16)
    hidden = jax.nn.relu(convolve(pooled, conv_first)).astype(jnp.bfloat16)
    return convolve(hidden, conv_second).astype(jnp.bfloat16)


def solution(mesh):
    in_specs = (
        P("groups", "tile", None, "date", None),
        P("groups", "tile", None, "date"),
        P(("groups", "date")),
        P("head"),
        P(None, "head"),
        P(None, "head"),
        P(None, None, None, "head"),
        P(None, None, None, "head"),
    )
    out_specs = P(("groups", "date"), "tile", None, "head")
    return jax.shard_map(local, mesh=mesh, in_specs=in_specs, out_specs=out_specs, check_vma=False)
```

profile of v0, /device:TPU:0, one launch (start us, length us, event | category | flops | bytes accessed | tf_op | source)
XLA Modules:
  0.0 57.5 jit_solution(14288607514884827071)
XLA Ops:
  0.0 0.9 %copy.23 = bf16[256,128]{0,1:T(8,128)(2,1)S(1)} copy(bf16[256,128]{1,0:T(8,128)(2,1)} %param.12) | data formatting | bytes 131072 | tf_op args[4]
  1.0 0.7 %mul.62 = f32[4,32]{1,0:T(4,128)S(1)} reshape(f32[128]{0:T(128)} %param.11) | data formatting | bytes 1024 | tf_op jit(solution)/shard_map/mul | solution.py:75
  2.4 0.8 %subtract_multiply_fusion = f32[4,4,8,16]{3,2,1,0:T(8,128)S(1)} fusion(s32[4,4,8,16]{3,2,1,0:T(8,128)} %param.9), kind=kLoop, calls=%fused_computation.79 | loop fusion | flops 6144 | bytes 16384 | tf_op jit(solution)/shard_map/mul | solution.py:76
  3.4 2.6 %multiply_reduce_fusion.1 = f32[4,4,8,16,4]{3,4,2,1,0:T(4,128)S(1)} fusion(bf16[4,32,256,1,1,1]{2,1,0,5,4,3:T(8,128)(2,1)S(1)} %bitcast.147, f32[4,32]{1,0:T(4,128)S(1)} %mul.62, bf16[4,4,8,16,256]{4,3,2,1,0:T(8,128)(2,1)} %param.8, f32[16,256]{1,0:T(8,128)S(1)} %fusion.47), kind=kOutput, calls=%fused_computation.1 | convolution fusion | flops 136306688 | bytes 1163776 | tf_op jit(solution)/shard_map/dot_general | solution.py:68
  6.4 0.7 %reshape.252 = f32[4,1,128]{2,1,0:T(1,128)} reshape(f32[4,4,4,8]{3,2,1,0:T(4,128)S(1)} %bitcast.146) | data formatting | bytes 4096
  7.1 6.3 %all-to-all-start.1 = ((f32[4,1,128]{2,1,0:T(1,128)}), f32[4,1,128]{2,1,0:T(1,128)S(1)}, u32[]{:S(2)}, u32[]{:S(2)}) async-start(f32[4,1,128]{2,1,0:T(1,128)} %reshape.252), calls=%async_computation.1 | async-start | bytes 4096 | tf_op jit(solution)/shard_map/all_to_all | solution.py:82
  14.0 1.4 %multiply_reduce_fusion = f32[4,4,8,4,32]{4,3,2,1,0:T(4,128)S(1)} fusion(bf16[4,32,256,1,1,1]{2,1,0,5,4,3:T(8,128)(2,1)S(1)} %bitcast.148, f32[4,4,8,16,4]{3,4,2,1,0:T(4,128)S(1)} %get-tuple-element.8, bf16[4,4,8,16,256]{4,3,2,1,0:T(8,128)(2,1)S(1)} %copy-done.3, f32[16,256]{1,0:T(8,128)S(1)} %fusion.47), kind=kOutput, calls=%fused_computation | convolution fusion | flops 136298496 | bytes 1228800 | tf_op jit(solution)/shard_map/dot_general | solution.py:71
  15.6 0.7 %reshape.250 = f32[4,1,128]{2,1,0:T(1,128)} reshape(f32[4,4,4,8]{3,2,1,0:T(4,128)S(1)} %bitcast.145) | data formatting | bytes 4096
  16.2 0.8 %reshape.228 = f32[4,4,8,128]{3,2,1,0:T(8,128)} reshape(f32[4,4,8,4,32]{4,3,2,1,0:T(4,128)S(1)} %multiply_reduce_fusion) | data formatting | bytes 131072 | tf_op jit(solution)/shard_map/reshape | solution.py:80
  17.0 1.9 %all-to-all-done.1 = f32[4,1,128]{2,1,0:T(1,128)S(1)} async-done(((f32[4,1,128]{2,1,0:T(1,128)}), f32[4,1,128]{2,1,0:T(1,128)S(1)}, u32[]{:S(2)}, u32[]{:S(2)}) %all-to-all-start.1) | async-done | bytes 2080 | tf_op jit(solution)/shard_map/all_to_all | solution.py:82
  18.9 3.2 %all-to-all-start.2 = ((f32[4,1,128]{2,1,0:T(1,128)}), f32[4,1,128]{2,1,0:T(1,128)S(1)}, u32[]{:S(2)}, u32[]{:S(2)}) async-start(f32[4,1,128]{2,1,0:T(1,128)} %reshape.250), calls=%async_computation.2 | async-start | bytes 4096 | tf_op jit(solution)/shard_map/all_to_all | solution.py:83
  23.4 4.1 %all-to-all-done.2 = f32[4,1,128]{2,1,0:T(1,128)S(1)} async-done(((f32[4,1,128]{2,1,0:T(1,128)}), f32[4,1,128]{2,1,0:T(1,128)S(1)}, u32[]{:S(2)}, u32[]{:S(2)}) %all-to-all-start.2) | async-done | bytes 2080 | tf_op jit(solution)/shard_map/all_to_all | solution.py:83
  27.5 3.3 %all-to-all-start = ((f32[4,4,8,128]{3,2,1,0:T(8,128)}), f32[4,4,8,128]{3,2,1,0:T(8,128)S(1)}, u32[]{:S(2)}, u32[]{:S(2)}) async-start(f32[4,4,8,128]{3,2,1,0:T(8,128)} %reshape.228), calls=%async_computation | async-start | bytes 131072 | tf_op jit(solution)/shard_map/all_to_all | solution.py:84
  30.8 0.7 %reduce.7 = f32[4,128]{1,0:T(4,128)S(1)} reduce(f32[4,1,128]{2,1,0:T(1,128)S(1)} %all-to-all-done.2, f32[]{:T(128)} %broadcast.137), dimensions={1}, to_apply=%all_to_all.11.reduce_sub_computation | reduce | bytes 4100 | tf_op jit(solution)/shard_map/all_to_all | solution.py:83
  32.5 4.1 %all-to-all-done = f32[4,4,8,128]{3,2,1,0:T(8,128)S(1)} async-done(((f32[4,4,8,128]{3,2,1,0:T(8,128)}), f32[4,4,8,128]{3,2,1,0:T(8,128)S(1)}, u32[]{:S(2)}, u32[]{:S(2)}) %all-to-all-start) | async-done | bytes 65568 | tf_op jit(solution)/shard_map/all_to_all | solution.py:84
  36.5 1.3 %collective-permute-start.1 = (bf16[1,1,8,128]{3,2,1,0:T(8,128)(2,1)S(1)}, bf16[1,1,8,128]{3,2,1,0:T(8,128)(2,1)S(1)}, u32[]{:S(2)}, u32[]{:S(2)}) collective-permute-start(bf16[1,1,8,128]{3,2,1,0:T(8,128)(2,1)S(1)} %get-tuple-element.12), channel_id=1, source_target_pairs={{2,0},{3,1},{6,4},{7,5},{10,8},{11,9},{14,12},{15,13},{18,16},{19,... | collective-permute-start | bytes 6152 | tf_op jit(solution)/shard_map/ppermute | solution.py:19
  37.8 4.5 %collective-permute-start = (bf16[1,1,8,128]{3,2,1,0:T(8,128)(2,1)S(1)}, bf16[1,1,8,128]{3,2,1,0:T(8,128)(2,1)S(1)}, u32[]{:S(2)}, u32[]{:S(2)}) collective-permute-start(bf16[1,1,8,128]{3,2,1,0:T(8,128)(2,1)S(1)} %get-tuple-element.11), channel_id=1, source_target_pairs={{0,2},{1,3},{4,6},{5,7},{8,10},{9,11},{12,14},{13,15},{16,18},{17,... | collective-permute-start | bytes 6152 | tf_op jit(solution)/shard_map/ppermute | solution.py:16
  42.4 1.3 %collective-permute-done = bf16[1,1,8,128]{3,2,1,0:T(8,128)(2,1)S(1)} collective-permute-done((bf16[1,1,8,128]{3,2,1,0:T(8,128)(2,1)S(1)}, bf16[1,1,8,128]{3,2,1,0:T(8,128)(2,1)S(1)}, u32[]{:S(2)}, u32[]{:S(2)}) %collective-permute-start) | collective-permute-done | bytes 2080 | tf_op jit(solution)/shard_map/ppermute | solution.py:16
  43.7 1.8 %all_gather.6 = bf16[1,6,8,256]{3,2,1,0:T(8,128)(2,1)S(1)} all-gather(bf16[1,6,8,128]{3,2,1,0:T(8,128)(2,1)S(1)} %pad_maximum_fusion), channel_id=1, replica_groups=mesh['groups'=2,'date'=4,'tile'=2,'head'=2] {'head'}, dimensions={3}, use_global_device_ids=true | all-gather | bytes 36864 | tf_op jit(solution)/shard_map/all_gather | solution.py:47
  46.7 1.3 %collective-permute-start.3 = (bf16[1,1,8,128]{3,2,1,0:T(8,128)(2,1)S(1)}, bf16[1,1,8,128]{3,2,1,0:T(8,128)(2,1)S(1)}, u32[]{:S(2)}, u32[]{:S(2)}) collective-permute-start(bf16[1,1,8,128]{3,2,1,0:T(8,128)(2,1)S(1)} %get-tuple-element.10), channel_id=1, source_target_pairs={{2,0},{3,1},{6,4},{7,5},{10,8},{11,9},{14,12},{15,13},{18,16},{19,... | collective-permute-start | bytes 6152 | tf_op jit(solution)/shard_map/ppermute | solution.py:19
  48.0 4.5 %collective-permute-start.2 = (bf16[1,1,8,128]{3,2,1,0:T(8,128)(2,1)S(1)}, bf16[1,1,8,128]{3,2,1,0:T(8,128)(2,1)S(1)}, u32[]{:S(2)}, u32[]{:S(2)}) collective-permute-start(bf16[1,1,8,128]{3,2,1,0:T(8,128)(2,1)S(1)} %get-tuple-element.9), channel_id=1, source_target_pairs={{0,2},{1,3},{4,6},{5,7},{8,10},{9,11},{12,14},{13,15},{16,18},{17,... | collective-permute-start | bytes 6152 | tf_op jit(solution)/shard_map/ppermute | solution.py:16
  52.6 1.3 %collective-permute-done.2 = bf16[1,1,8,128]{3,2,1,0:T(8,128)(2,1)S(1)} collective-permute-done((bf16[1,1,8,128]{3,2,1,0:T(8,128)(2,1)S(1)}, bf16[1,1,8,128]{3,2,1,0:T(8,128)(2,1)S(1)}, u32[]{:S(2)}, u32[]{:S(2)}) %collective-permute-start.2) | collective-permute-done | bytes 2080 | tf_op jit(solution)/shard_map/ppermute | solution.py:16
  53.9 1.8 %all_gather.7 = bf16[1,6,8,256]{3,2,1,0:T(8,128)(2,1)S(1)} all-gather(bf16[1,6,8,128]{3,2,1,0:T(8,128)(2,1)S(1)} %pad_maximum_fusion.1), channel_id=1, replica_groups=mesh['groups'=2,'date'=4,'tile'=2,'head'=2] {'head'}, dimensions={3}, use_global_device_ids=true | all-gather | bytes 36864 | tf_op jit(solution)/shard_map/all_gather | solution.py:47
  56.8 0.7 %fusion.3 = bf16[1,4,8,128]{3,2,1,0:T(8,128)(2,1)} fusion(f32[32,128]{1,0:T(8,128)S(1)} %convolution_add_fusion.1, bf16[3,3,256,128]{3,2,1,0:T(8,128)(2,1)S(1)} %copy-done.1, bf16[1,6,8,256]{3,2,1,0:T(8,128)(2,1)S(1)} %all_gather.7), kind=kOutput, calls=%fused_computation.22 | convolution fusion | flops 2105344 | bytes 114688 | tf_op jit(solution)/shard_map/dot_general | solution.py:53
  (54 shorter events, 6.5 us)
Async XLA Ops:
  6.0 7.8 %copy-start.2 = (bf16[256,128]{1,0:T(8,128)(2,1)S(1)}, bf16[256,128]{1,0:T(8,128)(2,1)}, u32[]{:S(2)}) copy-start(bf16[256,128]{1,0:T(8,128)(2,1)} %param.13) | copy-start | bytes 196612
  6.0 7.9 %copy-start.3 = (bf16[4,4,8,16,256]{4,3,2,1,0:T(8,128)(2,1)S(1)}, bf16[4,4,8,16,256]{4,3,2,1,0:T(8,128)(2,1)}, u32[]{:S(2)}) copy-start(bf16[4,4,8,16,256]{4,3,2,1,0:T(8,128)(2,1)} %param.8) | copy-start | bytes 3145732
  7.1 11.8 %all-to-all-start.1 = ((f32[4,1,128]{2,1,0:T(1,128)}), f32[4,1,128]{2,1,0:T(1,128)S(1)}, u32[]{:S(2)}, u32[]{:S(2)}) async-start(f32[4,1,128]{2,1,0:T(1,128)} %reshape.252), calls=%async_computation.1 | async-start | bytes 4096 | tf_op jit(solution)/shard_map/all_to_all | solution.py:82
  15.4 30.1 %copy-start = (bf16[3,3,256,128]{3,2,1,0:T(8,128)(2,1)S(1)}, bf16[3,3,256,128]{3,2,1,0:T(8,128)(2,1)}, u32[]{:S(2)}) copy-start(bf16[3,3,256,128]{3,2,1,0:T(8,128)(2,1)} %param.14) | copy-start | bytes 1769476
  18.9 8.6 %all-to-all-start.2 = ((f32[4,1,128]{2,1,0:T(1,128)}), f32[4,1,128]{2,1,0:T(1,128)S(1)}, u32[]{:S(2)}, u32[]{:S(2)}) async-start(f32[4,1,128]{2,1,0:T(1,128)} %reshape.250), calls=%async_computation.2 | async-start | bytes 4096 | tf_op jit(solution)/shard_map/all_to_all | solution.py:83
  27.5 9.0 %all-to-all-start = ((f32[4,4,8,128]{3,2,1,0:T(8,128)}), f32[4,4,8,128]{3,2,1,0:T(8,128)S(1)}, u32[]{:S(2)}, u32[]{:S(2)}) async-start(f32[4,4,8,128]{3,2,1,0:T(8,128)} %reshape.228), calls=%async_computation | async-start | bytes 131072 | tf_op jit(solution)/shard_map/all_to_all | solution.py:84
  31.9 23.8 %copy-start.1 = (bf16[3,3,256,128]{3,2,1,0:T(8,128)(2,1)S(1)}, bf16[3,3,256,128]{3,2,1,0:T(8,128)(2,1)}, u32[]{:S(2)}) copy-start(bf16[3,3,256,128]{3,2,1,0:T(8,128)(2,1)} %param.15) | copy-start | bytes 1769476
  36.5 5.9 %collective-permute-start.1 = (bf16[1,1,8,128]{3,2,1,0:T(8,128)(2,1)S(1)}, bf16[1,1,8,128]{3,2,1,0:T(8,128)(2,1)S(1)}, u32[]{:S(2)}, u32[]{:S(2)}) collective-permute-start(bf16[1,1,8,128]{3,2,1,0:T(8,128)(2,1)S(1)} %get-tuple-element.12), channel_id=1, source_target_pairs={{2,0},{3,1},{6,4},{7,5},{10,8},{11,9},{14,12},{15,13},{18,16},{19,... | collective-permute-start | bytes 6152 | tf_op jit(solution)/shard_map/ppermute | solution.py:19
  37.8 5.8 %collective-permute-start = (bf16[1,1,8,128]{3,2,1,0:T(8,128)(2,1)S(1)}, bf16[1,1,8,128]{3,2,1,0:T(8,128)(2,1)S(1)}, u32[]{:S(2)}, u32[]{:S(2)}) collective-permute-start(bf16[1,1,8,128]{3,2,1,0:T(8,128)(2,1)S(1)} %get-tuple-element.11), channel_id=1, source_target_pairs={{0,2},{1,3},{4,6},{5,7},{8,10},{9,11},{12,14},{13,15},{16,18},{17,... | collective-permute-start | bytes 6152 | tf_op jit(solution)/shard_map/ppermute | solution.py:16
  46.7 5.9 %collective-permute-start.3 = (bf16[1,1,8,128]{3,2,1,0:T(8,128)(2,1)S(1)}, bf16[1,1,8,128]{3,2,1,0:T(8,128)(2,1)S(1)}, u32[]{:S(2)}, u32[]{:S(2)}) collective-permute-start(bf16[1,1,8,128]{3,2,1,0:T(8,128)(2,1)S(1)} %get-tuple-element.10), channel_id=1, source_target_pairs={{2,0},{3,1},{6,4},{7,5},{10,8},{11,9},{14,12},{15,13},{18,16},{19,... | collective-permute-start | bytes 6152 | tf_op jit(solution)/shard_map/ppermute | solution.py:19
  48.0 5.8 %collective-permute-start.2 = (bf16[1,1,8,128]{3,2,1,0:T(8,128)(2,1)S(1)}, bf16[1,1,8,128]{3,2,1,0:T(8,128)(2,1)S(1)}, u32[]{:S(2)}, u32[]{:S(2)}) collective-permute-start(bf16[1,1,8,128]{3,2,1,0:T(8,128)(2,1)S(1)} %get-tuple-element.9), channel_id=1, source_target_pairs={{0,2},{1,3},{4,6},{5,7},{8,10},{9,11},{12,14},{13,15},{16,18},{17,... | collective-permute-start | bytes 6152 | tf_op jit(solution)/shard_map/ppermute | solution.py:16
where the time goes:
time: 58.1 us; the launch traced here: 57.5 us
  starting transfers between devices  24.5 us (42%)
  waiting for transfers between devices  12.6 us (22%)
  matrix products  7.09 us (12%)
  local copies, waits for them, and re-layouts  5.82 us (10%)
  other arithmetic  3.7 us (6%)
  blocking collectives  3.62 us (6%)
    ppermute x2, starting transfers between devices, with_halo(): lax.ppermute(lax.slice_in_dim(block, block.shape[dim] - width, None, axis...  9.08 us
    all_to_all x1, starting transfers between devices, local(): lax.all_to_all(top, 'date', split_axis=0, concat_axis=0, tiled=True)  6.32 us
    all_to_all x1, waiting for transfers between devices, local(): lax.all_to_all(totals, 'date', split_axis=0, concat_axis=0, tiled=True)  4.08 us
    all_to_all x1, waiting for transfers between devices, local(): lax.all_to_all(sums, 'date', split_axis=0, concat_axis=0, tiled=True)  4.05 us
    all_gather x2, blocking collectives, convolve(): whole = lax.all_gather(padded, 'head', axis=3, tiled=True)  3.62 us
    all_to_all x1, starting transfers between devices, local(): lax.all_to_all(sums, 'date', split_axis=0, concat_axis=0, tiled=True)  3.28 us
    all_to_all x1, starting transfers between devices, local(): lax.all_to_all(totals, 'date', split_axis=0, concat_axis=0, tiled=True)  3.2 us
    dot_general x18, matrix products, convolve(): jnp.dot(piece, kernel[arow, bcol], preferred_element_type=jnp.float32)  3.05 us
  transfers between devices with their start and end apart: 7, of which 5 were waited for; matrix products, arithmetic and copies ran while one was open for 11% of the time, Pallas kernels for 0%

commit v1 on v0

--- a/solution.py
+++ b/solution.py
@@ -6,6 +6,35 @@
 HSIZE = 32
 TILE_DEV = 1
 cloud_penalty = 6.0
+
+
+def _supply_lots_all(array_here, dim_no, my_tile):
+    arr_next, shaped = (array_here.shape[:dim_no], array_here.shape[dim_no + 1 :])
+    answer = jnp.moveaxis(array_here.reshape(*arr_next, my_tile, -1, *shaped), dim_no, 0)
+    return answer
+
+
+def _match_patch(m, row_dim):
+    z_new = list(m.shape[1:])
+    z_new[row_dim] *= m.shape[0]
+    back = jnp.moveaxis(m, 0, row_dim).reshape(z_new)
+    return back
+
+
+def _pack_grid(buf, axis_name, z_in, work_x):
+    local_part = lax.axis_size(axis_name)
+    fresh = lax.axis_index(axis_name)
+    prior, opened = (local_part, fresh)
+    row_out = _supply_lots_all(buf, z_in, prior)
+    series = [row_out[opened]]
+    for w in range(1, prior):
+        value_now = row_out[opened ^ w]
+        known = lax.ppermute(value_now, axis_name, [(d, d ^ w) for d in range(prior)])
+        series.append(known)
+    h_now = jnp.stack(series)
+    row_out = h_now[opened ^ jnp.arange(prior)]
+    mat_out = _match_patch(row_out, work_x)
+    return mat_out
 
 
 def with_halo(block, sides, width):
@@ -81,7 +110,7 @@
     got = (
         lax.all_to_all(top, "date", split_axis=0, concat_axis=0, tiled=True),
         lax.all_to_all(totals, "date", split_axis=0, concat_axis=0, tiled=True),
-        lax.all_to_all(sums, "date", split_axis=0, concat_axis=0, tiled=True),
+        _pack_grid(sums, "date", 0, 0),
     )
     sources = got[0].shape[0] // TILE_DEV
     tops = got[0].reshape(sources, TILE_DEV, rows, cols, heads_dev)

time: 58.1 us -> 55.2 us (0.950)
  waiting for transfers between devices: 12.6 us -> 6.67 us
  starting transfers between devices: 24.5 us -> 27.5 us
    ppermute x0 -> x3, starting transfers between devices: none -> 4.53 us  [_pack_grid(): lax.ppermute(value_now, axis_name, [(d, d ^ w) for d in range(prior)])]
    all_to_all x1 -> x0, waiting for transfers between devices: 4.05 us -> none  [local(): lax.all_to_all(sums, 'date', split_axis=0, concat_axis=0, tiled=True)]
    all_to_all x1 -> x0, starting transfers between devices: 3.28 us -> none  [local(): lax.all_to_all(sums, 'date', split_axis=0, concat_axis=0, tiled=True)]
    all_to_all x1, waiting for transfers between devices: 1.89 us -> 0.01 us  [local(): lax.all_to_all(top, 'date', split_axis=0, concat_axis=0, tiled=True)]
    all_to_all x1, starting transfers between devices: 3.2 us -> 5.01 us  [local(): lax.all_to_all(totals, 'date', split_axis=0, concat_axis=0, tiled=True)]
    reshape x1 -> x0, local copies, waits for them, and re-layouts: 0.78 us -> none  [local(): jnp.sum(expo[..., None] * vals, axis=3)]
  transfers between devices with their start and end apart: 7 -> 9, of which waited for: 5 -> 3; matrix products, arithmetic and copies ran while one was open for 11% -> 11% of each run, Pallas kernels for 0% -> 0%
where the time goes in v1:
time: 55.2 us; the launch traced here: 54.7 us
  starting transfers between devices  27.5 us (50%)
  matrix products  7.09 us (13%)
  waiting for transfers between devices  6.67 us (12%)
  local copies, waits for them, and re-layouts  5.8 us (11%)
  other arithmetic  3.72 us (7%)
  blocking collectives  3.62 us (7%)
    ppermute x2, starting transfers between devices, with_halo(): lax.ppermute(lax.slice_in_dim(block, block.shape[dim] - width, None, axis...  9.08 us
    all_to_all x1, starting transfers between devices, local(): lax.all_to_all(top, 'date', split_axis=0, concat_axis=0, tiled=True)  6.32 us
    all_to_all x1, starting transfers between devices, local(): lax.all_to_all(totals, 'date', split_axis=0, concat_axis=0, tiled=True)  5.01 us
    ppermute x3, starting transfers between devices, _pack_grid(): lax.ppermute(value_now, axis_name, [(d, d ^ w) for d in range(prior)])  4.53 us
    all_to_all x1, waiting for transfers between devices, local(): lax.all_to_all(totals, 'date', split_axis=0, concat_axis=0, tiled=True)  4.09 us
    all_gather x2, blocking collectives, convolve(): whole = lax.all_gather(padded, 'head', axis=3, tiled=True)  3.62 us
    dot_general x18, matrix products, convolve(): jnp.dot(piece, kernel[arow, bcol], preferred_element_type=jnp.float32)  3.05 us
    unnamed x14, local copies, waits for them, and re-layouts  2.67 us
  transfers between devices with their start and end apart: 9, of which 3 were waited for; matrix products, arithmetic and copies ran while one was open for 11% of the time, Pallas kernels for 0%

profile of v1, /device:TPU:0, one launch (start us, length us, event | category | flops | bytes accessed | tf_op | source)
XLA Modules:
  0.0 54.7 jit_solution(135719271481528787)
XLA Ops:
  0.0 0.9 %copy.23 = bf16[256,128]{0,1:T(8,128)(2,1)S(1)} copy(bf16[256,128]{1,0:T(8,128)(2,1)} %param.12) | data formatting | bytes 131072 | tf_op args[4]
  1.0 0.7 %mul.71 = f32[4,32]{1,0:T(4,128)S(1)} reshape(f32[128]{0:T(128)} %param.11) | data formatting | bytes 1024 | tf_op jit(solution)/shard_map/mul | solution.py:104
  1.7 0.7 %convert_element_type.63 = f32[16]{0:T(128)S(1)} convert(s32[16]{0:T(128)} %param.10) | non-fusion elementwise | flops 16 | bytes 128 | tf_op jit(solution)/shard_map/convert_element_type | solution.py:57
  2.4 0.8 %subtract_multiply_fusion = f32[4,4,8,16]{3,2,1,0:T(8,128)S(1)} fusion(s32[4,4,8,16]{3,2,1,0:T(8,128)} %param.9), kind=kLoop, calls=%fused_computation.82 | loop fusion | flops 6144 | bytes 16384 | tf_op jit(solution)/shard_map/mul | solution.py:105
  3.4 2.6 %multiply_reduce_fusion.1 = f32[4,4,8,16,4]{3,4,2,1,0:T(4,128)S(1)} fusion(bf16[4,32,256,1,1,1]{2,1,0,5,4,3:T(8,128)(2,1)S(1)} %bitcast.164, f32[4,32]{1,0:T(4,128)S(1)} %mul.71, bf16[4,4,8,16,256]{4,3,2,1,0:T(8,128)(2,1)} %param.8, f32[16,256]{1,0:T(8,128)S(1)} %fusion.48), kind=kOutput, calls=%fused_computation.2 | convolution fusion | flops 136306688 | bytes 1163776 | tf_op jit(solution)/shard_map/dot_general | solution.py:97
  6.4 0.7 %reshape.299 = f32[4,1,128]{2,1,0:T(1,128)} reshape(f32[4,4,4,8]{3,2,1,0:T(4,128)S(1)} %bitcast.163) | data formatting | bytes 4096
  7.1 6.3 %all-to-all-start = ((f32[4,1,128]{2,1,0:T(1,128)}), f32[4,1,128]{2,1,0:T(1,128)S(1)}, u32[]{:S(2)}, u32[]{:S(2)}) async-start(f32[4,1,128]{2,1,0:T(1,128)} %reshape.299), calls=%async_computation | async-start | bytes 4096 | tf_op jit(solution)/shard_map/all_to_all | solution.py:111
  14.0 1.4 %multiply_reduce_fusion = f32[4,4,8,4,32]{4,3,2,1,0:T(4,128)S(1)} fusion(bf16[4,32,256,1,1,1]{2,1,0,5,4,3:T(8,128)(2,1)S(1)} %bitcast.165, f32[4,4,8,16,4]{3,4,2,1,0:T(4,128)S(1)} %get-tuple-element.8, bf16[4,4,8,16,256]{4,3,2,1,0:T(8,128)(2,1)S(1)} %copy-done.3, f32[16,256]{1,0:T(8,128)S(1)} %fusion.48), kind=kOutput, calls=%fused_computation.1 | convolution fusion | flops 136298496 | bytes 1228800 | tf_op jit(solution)/shard_map/dot_general | solution.py:100
  15.6 3.9 %collective-permute-start.2 = (f32[1,4,8,128]{3,2,1,0:T(8,128)S(1)}, f32[1,4,8,128]{3,2,1,0:T(8,128)S(1)}, u32[]{:S(2)}, u32[]{:S(2)}) collective-permute-start(f32[1,4,8,128]{3,2,1,0:T(8,128)S(1)} %get-tuple-element.10), channel_id=1, source_target_pairs={{0,12},{4,8},{8,4},{12,0},{1,13},{5,9},{9,5},{13,1},{2,14},{6,10},... | collective-permute-start | bytes 49160 | tf_op jit(solution)/shard_map/ppermute | solution.py:32
  19.5 0.6 %collective-permute-start = (f32[1,4,8,128]{3,2,1,0:T(8,128)S(1)}, f32[1,4,8,128]{3,2,1,0:T(8,128)S(1)}, u32[]{:S(2)}, u32[]{:S(2)}) collective-permute-start(f32[1,4,8,128]{3,2,1,0:T(8,128)S(1)} %get-tuple-element.12), channel_id=1, source_target_pairs={{0,4},{4,0},{8,12},{12,8},{1,5},{5,1},{9,13},{13,9},{2,6},{6,2},{1... | collective-permute-start | bytes 49160 | tf_op jit(solution)/shard_map/ppermute | solution.py:32
  20.3 0.7 %reshape.297 = f32[4,1,128]{2,1,0:T(1,128)} reshape(f32[4,4,4,8]{3,2,1,0:T(4,128)S(1)} %bitcast.162) | data formatting | bytes 4096
  21.0 5.0 %all-to-all-start.1 = ((f32[4,1,128]{2,1,0:T(1,128)}), f32[4,1,128]{2,1,0:T(1,128)S(1)}, u32[]{:S(2)}, u32[]{:S(2)}) async-start(f32[4,1,128]{2,1,0:T(1,128)} %reshape.297), calls=%async_computation.1 | async-start | bytes 4096 | tf_op jit(solution)/shard_map/all_to_all | solution.py:112
  26.6 0.7 %reduce.9 = f32[4,128]{1,0:T(4,128)S(1)} reduce(f32[4,1,128]{2,1,0:T(1,128)S(1)} %all-to-all-done, f32[]{:T(128)} %broadcast.181), dimensions={1}, to_apply=%all_to_all.6.reduce_sub_computation | reduce | bytes 4100 | tf_op jit(solution)/shard_map/all_to_all | solution.py:111
  27.4 4.1 %all-to-all-done.1 = f32[4,1,128]{2,1,0:T(1,128)S(1)} async-done(((f32[4,1,128]{2,1,0:T(1,128)}), f32[4,1,128]{2,1,0:T(1,128)S(1)}, u32[]{:S(2)}, u32[]{:S(2)}) %all-to-all-start.1) | async-done | bytes 2080 | tf_op jit(solution)/shard_map/all_to_all | solution.py:112
  31.4 0.7 %reduce.10 = f32[4,128]{1,0:T(4,128)S(1)} reduce(f32[4,1,128]{2,1,0:T(1,128)S(1)} %all-to-all-done.1, f32[]{:T(128)} %broadcast.181), dimensions={1}, to_apply=%all_to_all.7.reduce_sub_computation | reduce | bytes 4100 | tf_op jit(solution)/shard_map/all_to_all | solution.py:112
  33.8 1.3 %collective-permute-start.4 = (bf16[1,1,8,128]{3,2,1,0:T(8,128)(2,1)S(1)}, bf16[1,1,8,128]{3,2,1,0:T(8,128)(2,1)S(1)}, u32[]{:S(2)}, u32[]{:S(2)}) collective-permute-start(bf16[1,1,8,128]{3,2,1,0:T(8,128)(2,1)S(1)} %get-tuple-element.16), channel_id=1, source_target_pairs={{2,0},{3,1},{6,4},{7,5},{10,8},{11,9},{14,12},{15,13},{18,16},{19,... | collective-permute-start | bytes 6152 | tf_op jit(solution)/shard_map/ppermute | solution.py:48
  35.1 4.5 %collective-permute-start.3 = (bf16[1,1,8,128]{3,2,1,0:T(8,128)(2,1)S(1)}, bf16[1,1,8,128]{3,2,1,0:T(8,128)(2,1)S(1)}, u32[]{:S(2)}, u32[]{:S(2)}) collective-permute-start(bf16[1,1,8,128]{3,2,1,0:T(8,128)(2,1)S(1)} %get-tuple-element.15), channel_id=1, source_target_pairs={{0,2},{1,3},{4,6},{5,7},{8,10},{9,11},{12,14},{13,15},{16,18},{17,... | collective-permute-start | bytes 6152 | tf_op jit(solution)/shard_map/ppermute | solution.py:45
  39.6 1.3 %collective-permute-done.3 = bf16[1,1,8,128]{3,2,1,0:T(8,128)(2,1)S(1)} collective-permute-done((bf16[1,1,8,128]{3,2,1,0:T(8,128)(2,1)S(1)}, bf16[1,1,8,128]{3,2,1,0:T(8,128)(2,1)S(1)}, u32[]{:S(2)}, u32[]{:S(2)}) %collective-permute-start.3) | collective-permute-done | bytes 2080 | tf_op jit(solution)/shard_map/ppermute | solution.py:45
  40.9 1.8 %all_gather.6 = bf16[1,6,8,256]{3,2,1,0:T(8,128)(2,1)S(1)} all-gather(bf16[1,6,8,128]{3,2,1,0:T(8,128)(2,1)S(1)} %pad_maximum_fusion), channel_id=1, replica_groups=mesh['groups'=2,'date'=4,'tile'=2,'head'=2] {'head'}, dimensions={3}, use_global_device_ids=true | all-gather | bytes 36864 | tf_op jit(solution)/shard_map/all_gather | solution.py:76
  43.9 1.3 %collective-permute-start.6 = (bf16[1,1,8,128]{3,2,1,0:T(8,128)(2,1)S(1)}, bf16[1,1,8,128]{3,2,1,0:T(8,128)(2,1)S(1)}, u32[]{:S(2)}, u32[]{:S(2)}) collective-permute-start(bf16[1,1,8,128]{3,2,1,0:T(8,128)(2,1)S(1)} %get-tuple-element.14), channel_id=1, source_target_pairs={{2,0},{3,1},{6,4},{7,5},{10,8},{11,9},{14,12},{15,13},{18,16},{19,... | collective-permute-start | bytes 6152 | tf_op jit(solution)/shard_map/ppermute | solution.py:48
  45.2 4.5 %collective-permute-start.5 = (bf16[1,1,8,128]{3,2,1,0:T(8,128)(2,1)S(1)}, bf16[1,1,8,128]{3,2,1,0:T(8,128)(2,1)S(1)}, u32[]{:S(2)}, u32[]{:S(2)}) collective-permute-start(bf16[1,1,8,128]{3,2,1,0:T(8,128)(2,1)S(1)} %get-tuple-element.13), channel_id=1, source_target_pairs={{0,2},{1,3},{4,6},{5,7},{8,10},{9,11},{12,14},{13,15},{16,18},{17,... | collective-permute-start | bytes 6152 | tf_op jit(solution)/shard_map/ppermute | solution.py:45
  49.8 1.3 %collective-permute-done.5 = bf16[1,1,8,128]{3,2,1,0:T(8,128)(2,1)S(1)} collective-permute-done((bf16[1,1,8,128]{3,2,1,0:T(8,128)(2,1)S(1)}, bf16[1,1,8,128]{3,2,1,0:T(8,128)(2,1)S(1)}, u32[]{:S(2)}, u32[]{:S(2)}) %collective-permute-start.5) | collective-permute-done | bytes 2080 | tf_op jit(solution)/shard_map/ppermute | solution.py:45
  51.1 1.8 %all_gather.7 = bf16[1,6,8,256]{3,2,1,0:T(8,128)(2,1)S(1)} all-gather(bf16[1,6,8,128]{3,2,1,0:T(8,128)(2,1)S(1)} %pad_maximum_fusion.1), channel_id=1, replica_groups=mesh['groups'=2,'date'=4,'tile'=2,'head'=2] {'head'}, dimensions={3}, use_global_device_ids=true | all-gather | bytes 36864 | tf_op jit(solution)/shard_map/all_gather | solution.py:76
  54.0 0.7 %fusion.3 = bf16[1,4,8,128]{3,2,1,0:T(8,128)(2,1)} fusion(f32[32,128]{1,0:T(8,128)S(1)} %convolution_add_fusion.1, bf16[3,3,256,128]{3,2,1,0:T(8,128)(2,1)S(1)} %copy-done.1, bf16[1,6,8,256]{3,2,1,0:T(8,128)(2,1)S(1)} %all_gather.7), kind=kOutput, calls=%fused_computation.23 | convolution fusion | flops 2105344 | bytes 114688 | tf_op jit(solution)/shard_map/dot_general | solution.py:82
  (63 shorter events, 5.9 us)
Async XLA Ops:
  6.0 7.9 %copy-start.2 = (bf16[256,128]{1,0:T(8,128)(2,1)S(1)}, bf16[256,128]{1,0:T(8,128)(2,1)}, u32[]{:S(2)}) copy-start(bf16[256,128]{1,0:T(8,128)(2,1)} %param.13) | copy-start | bytes 196612
  6.0 8.0 %copy-start.3 = (bf16[4,4,8,16,256]{4,3,2,1,0:T(8,128)(2,1)S(1)}, bf16[4,4,8,16,256]{4,3,2,1,0:T(8,128)(2,1)}, u32[]{:S(2)}) copy-start(bf16[4,4,8,16,256]{4,3,2,1,0:T(8,128)(2,1)} %param.8) | copy-start | bytes 3145732
  7.1 13.9 %all-to-all-start = ((f32[4,1,128]{2,1,0:T(1,128)}), f32[4,1,128]{2,1,0:T(1,128)S(1)}, u32[]{:S(2)}, u32[]{:S(2)}) async-start(f32[4,1,128]{2,1,0:T(1,128)} %reshape.299), calls=%async_computation | async-start | bytes 4096 | tf_op jit(solution)/shard_map/all_to_all | solution.py:111
  15.6 27.2 %copy-start = (bf16[3,3,256,128]{3,2,1,0:T(8,128)(2,1)S(1)}, bf16[3,3,256,128]{3,2,1,0:T(8,128)(2,1)}, u32[]{:S(2)}) copy-start(bf16[3,3,256,128]{3,2,1,0:T(8,128)(2,1)} %param.14) | copy-start | bytes 1769476
  15.6 17.5 %collective-permute-start.2 = (f32[1,4,8,128]{3,2,1,0:T(8,128)S(1)}, f32[1,4,8,128]{3,2,1,0:T(8,128)S(1)}, u32[]{:S(2)}, u32[]{:S(2)}) collective-permute-start(f32[1,4,8,128]{3,2,1,0:T(8,128)S(1)} %get-tuple-element.10), channel_id=1, source_target_pairs={{0,12},{4,8},{8,4},{12,0},{1,13},{5,9},{9,5},{13,1},{2,14},{6,10},... | collective-permute-start | bytes 49160 | tf_op jit(solution)/shard_map/ppermute | solution.py:32
  19.5 13.6 %collective-permute-start.1 = (f32[1,4,8,128]{3,2,1,0:T(8,128)S(1)}, f32[1,4,8,128]{3,2,1,0:T(8,128)S(1)}, u32[]{:S(2)}, u32[]{:S(2)}) collective-permute-start(f32[1,4,8,128]{3,2,1,0:T(8,128)S(1)} %get-tuple-element.11), channel_id=1, source_target_pairs={{0,8},{4,12},{8,0},{12,4},{1,9},{5,13},{9,1},{13,5},{2,10},{6,14},... | collective-permute-start | bytes 49160 | tf_op jit(solution)/shard_map/ppermute | solution.py:32
  19.5 13.6 %collective-permute-start = (f32[1,4,8,128]{3,2,1,0:T(8,128)S(1)}, f32[1,4,8,128]{3,2,1,0:T(8,128)S(1)}, u32[]{:S(2)}, u32[]{:S(2)}) collective-permute-start(f32[1,4,8,128]{3,2,1,0:T(8,128)S(1)} %get-tuple-element.12), channel_id=1, source_target_pairs={{0,4},{4,0},{8,12},{12,8},{1,5},{5,1},{9,13},{13,9},{2,6},{6,2},{1... | collective-permute-start | bytes 49160 | tf_op jit(solution)/shard_map/ppermute | solution.py:32
  21.0 10.4 %all-to-all-start.1 = ((f32[4,1,128]{2,1,0:T(1,128)}), f32[4,1,128]{2,1,0:T(1,128)S(1)}, u32[]{:S(2)}, u32[]{:S(2)}) async-start(f32[4,1,128]{2,1,0:T(1,128)} %reshape.297), calls=%async_computation.1 | async-start | bytes 4096 | tf_op jit(solution)/shard_map/all_to_all | solution.py:112
  32.9 20.0 %copy-start.1 = (bf16[3,3,256,128]{3,2,1,0:T(8,128)(2,1)S(1)}, bf16[3,3,256,128]{3,2,1,0:T(8,128)(2,1)}, u32[]{:S(2)}) copy-start(bf16[3,3,256,128]{3,2,1,0:T(8,128)(2,1)} %param.15) | copy-start | bytes 1769476
  33.8 5.9 %collective-permute-start.4 = (bf16[1,1,8,128]{3,2,1,0:T(8,128)(2,1)S(1)}, bf16[1,1,8,128]{3,2,1,0:T(8,128)(2,1)S(1)}, u32[]{:S(2)}, u32[]{:S(2)}) collective-permute-start(bf16[1,1,8,128]{3,2,1,0:T(8,128)(2,1)S(1)} %get-tuple-element.16), channel_id=1, source_target_pairs={{2,0},{3,1},{6,4},{7,5},{10,8},{11,9},{14,12},{15,13},{18,16},{19,... | collective-permute-start | bytes 6152 | tf_op jit(solution)/shard_map/ppermute | solution.py:48
  35.1 5.8 %collective-permute-start.3 = (bf16[1,1,8,128]{3,2,1,0:T(8,128)(2,1)S(1)}, bf16[1,1,8,128]{3,2,1,0:T(8,128)(2,1)S(1)}, u32[]{:S(2)}, u32[]{:S(2)}) collective-permute-start(bf16[1,1,8,128]{3,2,1,0:T(8,128)(2,1)S(1)} %get-tuple-element.15), channel_id=1, source_target_pairs={{0,2},{1,3},{4,6},{5,7},{8,10},{9,11},{12,14},{13,15},{16,18},{17,... | collective-permute-start | bytes 6152 | tf_op jit(solution)/shard_map/ppermute | solution.py:45
  43.9 5.9 %collective-permute-start.6 = (bf16[1,1,8,128]{3,2,1,0:T(8,128)(2,1)S(1)}, bf16[1,1,8,128]{3,2,1,0:T(8,128)(2,1)S(1)}, u32[]{:S(2)}, u32[]{:S(2)}) collective-permute-start(bf16[1,1,8,128]{3,2,1,0:T(8,128)(2,1)S(1)} %get-tuple-element.14), channel_id=1, source_target_pairs={{2,0},{3,1},{6,4},{7,5},{10,8},{11,9},{14,12},{15,13},{18,16},{19,... | collective-permute-start | bytes 6152 | tf_op jit(solution)/shard_map/ppermute | solution.py:48
  45.2 5.8 %collective-permute-start.5 = (bf16[1,1,8,128]{3,2,1,0:T(8,128)(2,1)S(1)}, bf16[1,1,8,128]{3,2,1,0:T(8,128)(2,1)S(1)}, u32[]{:S(2)}, u32[]{:S(2)}) collective-permute-start(bf16[1,1,8,128]{3,2,1,0:T(8,128)(2,1)S(1)} %get-tuple-element.13), channel_id=1, source_target_pairs={{0,2},{1,3},{4,6},{5,7},{8,10},{9,11},{12,14},{13,15},{16,18},{17,... | collective-permute-start | bytes 6152 | tf_op jit(solution)/shard_map/ppermute | solution.py:45
